TPU v7x, 512 devices: a whole 4x4x16 slice. The times are simulated.
512 devices in a mesh: rows: 16 (over z_hi, x, core), labels: 32 (over y, z_lo).
Axes of the slice: x: 4, y: 4, z: 16 (z_hi: 2, z_lo: 8; z = z_hi * 8 + z_lo), core: 2. Of those that a mesh axis runs over, the one named last changes fastest.
Arguments:
- pool_features: bfloat16 [2048, 768], P('rows'), may hold values from -6 to 6
- pool_labels: int32 [2048, 16], P('rows'), may hold values from 0 to 196607
- pool_counts: int32 [2048], P('rows'), may hold values from 1 to 16
- batch_rows: int32 [2, 512], P(None, 'rows'), may hold values from 0 to 127
- weights: float32 [196608, 768], P(('rows', 'labels')), may hold values from -0.21875 to 0.21875
- momentum: float32 [196608, 768], P(('rows', 'labels')), may hold values from -24 to 24
Outputs:
- new_weights: float32 [196608, 768], P(('rows', 'labels'))
- new_momentum: float32 [196608, 768], P(('rows', 'labels'))
- feature_grads: float32 [2, 512, 768], P(None, 'rows')
Inputs may be any that keep to these rules, and one draw needn't show every extreme that they name: `pool_labels`: slots of a list at or past its count are padding and are ignored; a label may appear twice in a list. `batch_rows`: an entry names one of the 128 examples stored with the index of rows that owns that batch row.
All inputs are finite; a program needn't handle non-finite values.
Results may differ from a plain program's by a relative error of at most 0.00045.
The roundings to bfloat16 on the way count: a program that leaves them out, or rounds other values in their place, can miss the bound.
Values may be sent and summed in bfloat16 or wider, within the bound.
A program may use at most 64 MiB of HBM per device.

v0:
```python
import math

import jax
import jax.numpy as jnp
from jax import lax
from jax.sharding import PartitionSpec as P

learn_rate = 0.001
decay_rate = 0.9


def side_by_side(arrays, axis, dim, along):
    widths = [math.prod(a.shape[along:]) for a in arrays]
    both = jnp.concatenate(
        [a.reshape(*a.shape[:along], w) for a, w in zip(arrays, widths)], axis=along
    )
    filled = lax.all_gather(both, axis, axis=dim, tiled=True)
    tiles = jnp.split(filled, [sum(widths[:k]) for k in range(1, len(widths))], axis=along)
    return tuple(
        (b.reshape(*filled.shape[:along], *a.shape[along:]) for a, b in zip(arrays, tiles))
    )


def feature_sums(errors_list, lowered_list, group_rows, width):
    parts = []
    for errors, low_weights in zip(errors_list, lowered_list):
        parts.append(jnp.dot(errors, low_weights, preferred_element_type=jnp.float32))
    whole = lax.psum(jnp.concatenate(parts, axis=1), ("rows", "labels"))
    mine = lax.dynamic_slice_in_dim(whole, lax.axis_index("rows") * group_rows, group_rows, 0)
    return jnp.stack([mine[:, :width], mine[:, width:]])


def per_device(pool_features, pool_labels, pool_counts, batch_rows, weights, momentum):
    lab_rows = weights.shape[0]
    group_rows = batch_rows.shape[1]
    width = weights.shape[1]
    device_index = lax.axis_index("rows") * lax.axis_size("labels") + lax.axis_index("labels")
    labels = device_index * lab_rows + jnp.arange(lab_rows, dtype=jnp.int32)
    all_ids, all_counts = side_by_side(
        (pool_labels[batch_rows], pool_counts[batch_rows]), "rows", 1, 2
    )
    all_features = lax.all_gather(pool_features[batch_rows], "rows", axis=1, tiled=True)
    errors_list = []
    lowered_list = []
    for batch in range(2):
        features = all_features[batch]
        label_ids = all_ids[batch]
        in_list = (
            jnp.arange(label_ids.shape[1], dtype=jnp.int32)[None, :] < all_counts[batch][:, None]
        )
        matched = (label_ids[:, :, None] == labels[None, None, :]) & in_list[:, :, None]
        targets = jnp.any(matched, axis=1).astype(jnp.float32)
        low_weights = weights.astype(jnp.bfloat16)
        logits = lax.dot_general(
            features, low_weights, (((1,), (1,)), ((), ())), preferred_element_type=jnp.float32
        )
        errors = (jax.nn.sigmoid(logits) - targets).astype(jnp.bfloat16)
        grads = lax.dot_general(
            errors, features, (((0,), (0,)), ((), ())), preferred_element_type=jnp.float32
        )
        errors_list.append(errors)
        lowered_list.append(low_weights)
        momentum = decay_rate * momentum + grads
        weights = weights - learn_rate * momentum
    return (weights, momentum, feature_sums(errors_list, lowered_list, group_rows, width))


def solution(mesh):
    in_specs = (
        P("rows", None),
        P("rows", None),
        P("rows"),
        P(None, "rows"),
        P(("rows", "labels"), None),
        P(("rows", "labels"), None),
    )
    out_specs = (P(("rows", "labels"), None), P(("rows", "labels"), None), P(None, "rows", None))
    return jax.shard_map(
        per_device, mesh=mesh, in_specs=in_specs, out_specs=out_specs, check_vma=False
    )
```

profile of v0, /device:TPU:24, one launch (start us, length us, event | category | flops | bytes accessed | tf_op | source)
XLA Modules:
  0.0 595.8 jit_solution(10529048860126078827)
XLA Ops:
  7.2 0.7 compare_select_fusion
  8.1 1.3 gather_fusion
  9.5 0.8 gather_fusion.2
  10.4 0.1 copy.21
  10.5 0.1 copy.19
  10.6 0.6 gather_fusion.1
  11.4 51.9 %all_gather.7 = s32[2,512,17]{2,0,1:T(2,128)S(1)} all-gather(s32[2,32,17]{2,0,1:T(2,128)S(1)} %pad_add_fusion), channel_id=1, replica_groups=mesh['rows'=16,'labels'=32] {'rows'}, dimensions={1}, use_global_device_ids=true | all-gather | bytes 73984 | tf_op jit(solution)/shard_map/all_gather | solution.py:17
  63.3 19.6 %slice_reduce_fusion = (s32[512]{0:T(512)S(1)}, s32[512]{0:T(512)S(1)}) fusion(s32[2,512,17]{2,0,1:T(2,128)S(1)} %all_gather.7), kind=kLoop, calls=%fused_computation.28 | loop fusion | bytes 8192 | tf_op jit(solution)/shard_map/slice | solution.py:49
  83.0 0.2 iota_compare_fusion
  83.2 0.4 fusion.14
  83.6 8.2 %and_reduce_fusion = (pred[512,384]{1,0:T(8,128)(4,1)S(1)}, pred[512,384]{1,0:T(8,128)(4,1)S(1)}) fusion(s32[512,16]{1,0:T(8,128)S(1)} %bitcast.27, s32[384]{0:T(512)S(1)} %iota_add_fusion, pred[512,16]{1,0:T(8,128)(4,1)S(1)} %get-tuple-element.15, pred[512,16]{1,0:T(8,128)(4,1)S(1)} %get-tuple-element.16, s32[512,16]{1,0:T(8,128)S(1)} %bitcast.26), kind=kLoop, calls=%fused_computation.3 | loop fusion | flops 18481152 | bytes 476672 | tf_op jit(solution)/shard_map/reduce_or | solution.py:52
  91.7 11.7 %all-gather.3.cloned.1.call-done = bf16[2,512,768]{2,1,0:T(8,128)(2,1)} async-done(((bf16[2,32,768]{2,1,0:T(8,128)(2,1)}), bf16[2,512,768]{2,1,0:T(8,128)(2,1)}) %all-gather.3.cloned.1.call-update) | async-done | bytes 1572880 | tf_op jit(solution)/shard_map/all_gather | solution.py:42
  103.4 1.8 fusion.9
  105.3 0.6 fusion.11
  105.8 0.8 copy-done.3
  106.6 0.3 copy-done.4
  107.0 0.6 fusion.10
  107.5 0.7 fusion.8
  108.2 0.6 fusion.15
  108.8 2.1 pad_maximum_fusion
  110.9 3.2 multiply_subtract_fusion
  114.0 473.3 %all-reduce.2.cloned.1.call-done = f32[512,1536]{1,0:T(8,128)} async-done(((f32[512,1536]{1,0:T(8,128)}), f32[512,1536]{1,0:T(8,128)}) %all-reduce.2.cloned.1.call-update) | async-done | bytes 3145744 | tf_op jit(solution)/shard_map/psum | solution.py:28
  587.3 1.0 dynamic-slice_bitcast_fusion.1
  588.2 0.7 pad_maximum_fusion.1
  (20 shorter events, 0.5 us)
Async XLA Ops:
  7.2 0.9 copy-start
  7.2 2.3 copy-start.1
  7.2 3.3 copy-start.5
  7.2 96.2 %all-gather.3.cloned.1.call-start = ((), (), s32[]{:S(2)}) async-start(), calls=%async_computation.1 | async-start | bytes 1671168 | tf_op jit(solution)/shard_map/all_gather | solution.py:42
  9.5 577.8 %all-reduce.2.cloned.1.call-start = ((), (), s32[]{:S(2)}) async-start(), calls=%async_computation | async-start | bytes 6291456 | tf_op jit(solution)/shard_map/psum | solution.py:28
  11.4 92.1 %copy-start.2 = (f32[384,768]{1,0:T(8,128)S(1)}, f32[384,768]{1,0:T(8,128)}, u32[]{:S(2)}) copy-start(f32[384,768]{1,0:T(8,128)} %param.10) | copy-start | bytes 3538948
  105.2 1.4 copy-start.3
  105.2 1.7 copy-start.4
Sparse Core Ops, SparseCore 0:
  12.0 91.4 all-gather.2
  111.0 476.2 all-reduce.1
where the time goes:
time: 596 us
  waiting for transfers between devices  485 us (81%)
  blocking collectives  51.9 us (9%)
  local copies, waits for them, and re-layouts  25.3 us (4%)
  between operations  14.2 us (2%)
  other arithmetic  12 us (2%)
  matrix products  7.3 us (1%)
    psum x1, waiting for transfers between devices, feature_sums(): whole = lax.psum(jnp.concatenate(parts, axis=1), ('rows', 'labels'))  473 us
    all_gather x1, blocking collectives, side_by_side(): filled = lax.all_gather(both, axis, axis=dim, tiled=True)  51.9 us
    slice x1, local copies, waits for them, and re-layouts, per_device(): all_counts[batch][:, None]  19.6 us
  transfers between devices with their start and end apart: 2, of which 2 were waited for; matrix products, arithmetic and copies ran while one was open for 6% of the time, Pallas kernels for 0%

commit v1 on v0

v1 whole, which is shorter than its diff:
```python
import jax
import jax.numpy as jnp
from jax import lax
from jax.experimental import pallas as pl
from jax.experimental.pallas import tpu as pltpu
from jax.sharding import PartitionSpec as P

learn_rate = 0.001
decay_rate = 0.9
MESH = pl.DeviceIdType.MESH
F32, BF16 = jnp.float32, jnp.bfloat16

NX, NY, WIDTH, TAIL, LAB, GRP = 4, 4, 768, 128, 384, 32
FULL = WIDTH + TAIL
COUNT_LANE = 48


def one_hot(cond):
    return jnp.where(cond, 1.0, 0.0).astype(BF16)


def iota(shape, dim):
    return lax.broadcasted_iota(jnp.int32, shape, dim)


def dot(a, b, dims):
    return lax.dot_general(a, b, (dims, ((), ())), preferred_element_type=F32)


def kernel(
    pool, labels, counts, batch_rows, w_in, m_in,
    w_out, m_out, fg_out,
    feats, w, m, low, logits, errs, grads, own_part, other_part, core_in, chip_sum,
    plane_in, quarter, line_in, line_sum, far_in, result,
    x_send, x_recv, edge_send, edge_recv, core_send, core_recv, part_send, part_recv,
    plane_send, plane_recv, line_send, line_recv, far_send, far_recv, all_send, all_recv, local,
):
    rows_at, labels_at = lax.axis_index("rows"), lax.axis_index("labels")
    zh, x, c = rows_at >> 3, (rows_at >> 1) & 3, rows_at & 1
    y, zl = labels_at >> 3, labels_at & 7
    z = zh * 8 + zl
    a, b = z >> 2, z & 3
    edge = (zl == 0) | (zl == 7)
    holder = zh == (y >> 1)
    pending = []

    def device(x=x, y=y, z=z, c=c):
        z = z & 15
        return ((z >> 3) * 8 + x * 2 + c, y * 8 + (z & 7))

    def remote(src, dst, send, recv, to):
        return pltpu.make_async_remote_copy(
            src_ref=src, dst_ref=dst, send_sem=send, recv_sem=recv,
            device_id=to, device_id_type=MESH,
        )

    def start(*args, when=None):
        def go():
            remote(*args).start()

        def done():
            remote(*args).wait_send()

        pending.append((done, when))
        if when is None:
            go()
        else:
            pl.when(when)(go)

    def arrived(dst, recv):
        remote(dst, dst, recv, recv, device(c=1 - c)).wait_recv()

    barrier = pltpu.get_barrier_semaphore()

    def greet(to):
        pl.semaphore_signal(barrier, inc=1, device_id=to, device_id_type=MESH)

    source_z = jnp.where(zl < 4, zh * 8 + 15, zh * 8 + 8)
    greet(device(z=source_z))
    greet(device(c=1 - c))
    for p in range(1, 16):
        greet(device(x=(x + (p >> 2)) & 3, y=(y + (p & 3)) & 3))
    for d in range(1, 4):
        greet(device(z=a * 4 + ((b + d) & 3)))
    for i in range(2):
        for k in range(4):
            from_y = 2 * zh + i

            @pl.when((from_y != y) | (k != b))
            def _():
                greet(device(y=from_y, z=a * 4 + k))

    @pl.when(holder)
    def _():
        for d in range(1, 4):
            greet(device(z=z + 4 * d))

    load_w = pltpu.make_async_copy(w_in, w, local.at[0])
    load_m = pltpu.make_async_copy(m_in, m, local.at[1])
    load_w.start()
    load_m.start()

    lists = labels[...]
    tail = jnp.zeros((128, TAIL), F32)
    for d in range(3):
        digit = ((lists >> (6 * d)) & 63).astype(F32).astype(BF16)
        place = one_hot(iota((16, TAIL), 0) + 16 * d == iota((16, TAIL), 1))
        tail = tail + dot(digit, place, ((1,), (0,)))
    on_diagonal = iota((128, 128), 0) == iota((128, 128), 1)
    diagonal = jnp.where(on_diagonal, counts[...].astype(F32), 0.0).astype(BF16)
    tail = tail + dot(diagonal, one_hot(iota((128, TAIL), 1) == COUNT_LANE), ((1,), (0,)))
    tail = tail.astype(BF16)
    for t in range(2):
        chosen = one_hot(iota((128, GRP), 0) == batch_rows[pl.ds(t, 1), :])
        own = feats.at[t, 0, 0, x]
        own[:, :WIDTH] = dot(chosen, pool[...], ((0,), (0,))).astype(BF16)
        own[:, WIDTH:] = dot(chosen, tail, ((0,), (0,))).astype(BF16)

    pl.semaphore_wait(
        barrier, 19 + jnp.where(holder, 16, 2) + jnp.where(edge, 4, 0)
    )

    def send_edge(t):
        for k in (3, 2, 1, 0):
            to_z = jnp.where(zl == 0, z - 1 - k, z + 1 + k)
            start(
                feats.at[t, 0, 0, x], feats.at[t, 1, 0, x],
                edge_send.at[t, k], edge_recv.at[t], device(z=to_z), when=edge,
            )

    def send_core(t, far, at):
        start(
            feats.at[t, far, 0, at], feats.at[t, far, 1, at],
            core_send.at[t, far, at], core_recv.at[t, far, at], device(c=1 - c),
        )

    def send_x(t, far):
        for d in (2, 1, 3):
            start(
                feats.at[t, far, 0, x], feats.at[t, far, 0, x],
                x_send.at[t, far, d - 1], x_recv.at[t, far, d - 1], device(x=(x + d) & 3),
            )
        send_core(t, far, x)

    def pass_on(t, far):
        for d in (1, 3, 2):
            at = (x - d) & 3
            arrived(feats.at[t, far, 0, at], x_recv.at[t, far, d - 1])
            send_core(t, far, at)

    def have_edge(t):
        arrived(feats.at[t, 1, 0, x], edge_recv.at[t])
        send_x(t, 1)

    def have_core(t, far):
        for at in range(NX):
            arrived(feats.at[t, far, 1, at], core_recv.at[t, far, at])

    base = ((rows_at * 32 + labels_at) * LAB).astype(F32)

    def block_errors(t, far):
        block = feats[t, far].reshape(8 * GRP, FULL)
        features, lists = block[:, :WIDTH], block[:, WIDTH:]
        logits[...] = dot(low[t], features, ((1,), (1,)))
        slot, lane = iota((16, TAIL), 0), iota((16, TAIL), 1)
        weight = jnp.zeros((16, TAIL), F32)
        for d in range(3):
            weight = jnp.where(lane == slot + 16 * d, float(64**d), weight)
        ids = dot(weight.astype(BF16), lists, ((1,), (1,)))
        used = dot(one_hot(lane == COUNT_LANE), lists, ((1,), (1,)))
        in_list = iota(ids.shape, 0).astype(F32) < used
        ids = jnp.where(in_list, ids - base, -1.0)

        def chunk(i, _):
            at = pl.ds(pl.multiple_of(i * 64, 64), 64)
            label = (iota((64, 8 * GRP), 0) + i * 64).astype(F32)
            hit = ids[0:1, :] == label
            for k in range(1, 16):
                hit = hit | (ids[k : k + 1, :] == label)
            targets = jnp.where(hit, 1.0, 0.0)
            errs[t, far, at, :] = (jax.nn.sigmoid(logits[at, :]) - targets).astype(BF16)
            return 0

        lax.fori_loop(0, LAB // 64, chunk, 0)
        part = dot(errs[t, far], features, ((1,), (0,)))
        if far:
            grads[...] += part
        else:
            grads[...] = part

    def update(t):
        def chunk(i, _):
            at = pl.ds(pl.multiple_of(i * 64, 64), 64)
            moment = decay_rate * m[at, :] + grads[at, :]
            weight = w[at, :] - learn_rate * moment
            m[at, :] = moment
            w[at, :] = weight
            if t == 0:
                low[1, at, :] = weight.astype(BF16)
            return 0

        lax.fori_loop(0, LAB // 64, chunk, 0)

    def products(t):
        for other in (1, 0):
            cols = pl.ds(other * 128, 128)
            both = jnp.concatenate([errs[t, 0, :, cols], errs[t, 1, :, cols]], axis=1)
            part = dot(both, low[t], ((0,), (0,))).reshape(2, NX, 2, 16, WIDTH)
            if other:
                other_part[t] = part
                start(
                    other_part.at[t], core_in.at[t],
                    part_send.at[t], part_recv.at[t], device(c=1 - c),
                )
            else:
                own_part[t] = part

    def plane_start(t):
        arrived(core_in.at[t], part_recv.at[t])

        def chunk(i, _):
            far, at = i >> 2, i & 3
            chip_sum[t, far, at] = (own_part[t, far, at] + core_in[t, far, at]).astype(BF16)
            return 0

        lax.fori_loop(0, 8, chunk, 0)
        for p in range(1, 16):
            to_x, to_y = (x + (p >> 2)) & 3, (y + (p & 3)) & 3
            start(
                chip_sum.at[t, (to_y >> 1) ^ zh, to_x, to_y & 1], plane_in.at[t, p - 1],
                plane_send.at[t, p - 1], plane_recv.at[t, p - 1], device(x=to_x, y=to_y),
            )

    def line_start(t):
        mine = (t, (y >> 1) ^ zh, x, y & 1)
        total = own_part[mine] + core_in[mine]
        for p in range(1, 16):
            arrived(plane_in.at[t, p - 1], plane_recv.at[t, p - 1])
        for p in range(1, 16):
            total = total + plane_in[t, p - 1].astype(F32)
        for k in range(4):
            quarter[t, k] = total[8 * (k >> 1) : 8 * (k >> 1) + 8, 384 * (k & 1) : 384 * (k & 1) + 384]
        for d in range(1, 4):
            to_b = (b + d) & 3
            start(
                quarter.at[t, to_b], line_in.at[t, d - 1],
                line_send.at[t, d - 1], line_recv.at[t, d - 1], device(z=a * 4 + to_b),
            )

    def far_start(t):
        total = quarter[t, b]
        for d in range(1, 4):
            arrived(line_in.at[t, d - 1], line_recv.at[t, d - 1])
            total = total + line_in[t, d - 1]
        line_sum[t] = total
        for d in (2, 1, 3):
            start(
                line_sum.at[t], far_in.at[t, d - 1], far_send.at[t, d - 1], far_recv.at[t, d - 1],
                device(z=z + 4 * d), when=(((a + d) & 3) >> 1) == (y >> 1),
            )

    def all_start(t):
        @pl.when(holder)
        def _():
            total = line_sum[t]
            for d in range(1, 4):
                arrived(far_in.at[t, d - 1], far_recv.at[t, d - 1])
                total = total + far_in[t, d - 1]
            result[t, y & 1, b] = total

        for q in range(15, 0, -1):
            start(
                result.at[t, y & 1, b], result.at[t, y & 1, b],
                all_send.at[t, q - 1], all_recv.at[t, y & 1, b],
                device(y=(y + (q >> 2)) & 3, z=a * 4 + ((b + (q & 3)) & 3)), when=holder,
            )

    def finish(t):
        for i in range(2):
            for k in range(4):
                mine = holder & (i == (y & 1)) & (k == b)

                @pl.when(jnp.logical_not(mine))
                def _():
                    arrived(result.at[t, i, k], all_recv.at[t, i, k])

        for i in range(2):
            for k in range(4):
                r, s = 16 * i + 8 * (k >> 1), 384 * (k & 1)
                fg_out[t, r : r + 8, s : s + 384] = result[t, i, k]

    send_edge(0)
    send_x(0, 0)
    send_x(1, 0)
    load_w.wait()
    load_m.wait()
    low[0] = w[...].astype(BF16)
    pass_on(0, 0)
    send_edge(1)
    have_edge(0)
    have_core(0, 0)
    block_errors(0, 0)
    pass_on(1, 0)
    pass_on(0, 1)
    have_core(0, 1)
    block_errors(0, 1)
    update(0)
    have_edge(1)
    products(0)
    have_core(1, 0)
    block_errors(1, 0)
    pass_on(1, 1)
    plane_start(0)
    have_core(1, 1)
    block_errors(1, 1)
    products(1)
    line_start(0)
    plane_start(1)
    update(1)
    store_w = pltpu.make_async_copy(w, w_out, local.at[2])
    store_m = pltpu.make_async_copy(m, m_out, local.at[3])
    store_w.start()
    store_m.start()
    far_start(0)
    line_start(1)
    all_start(0)
    far_start(1)
    all_start(1)
    finish(0)
    finish(1)
    for done, when in pending:
        if when is None:
            done()
        else:
            pl.when(when)(done)
    store_w.wait()
    store_m.wait()


def per_device(pool_features, pool_labels, pool_counts, batch_rows, weights, momentum):
    vmem, anywhere = pl.BlockSpec(memory_space=pltpu.VMEM), pl.BlockSpec(memory_space=pl.ANY)
    dma = pltpu.SemaphoreType.DMA
    part = (2, 2, NX, 2, 16, WIDTH)
    return pl.pallas_call(
        kernel,
        out_shape=(
            jax.ShapeDtypeStruct(weights.shape, F32),
            jax.ShapeDtypeStruct(momentum.shape, F32),
            jax.ShapeDtypeStruct((2, GRP, WIDTH), F32),
        ),
        in_specs=[vmem, vmem, vmem, vmem, anywhere, anywhere],
        out_specs=(anywhere, anywhere, vmem),
        scratch_shapes=[
            pltpu.VMEM((2, 2, 2, NX, GRP, FULL), BF16),
            pltpu.VMEM((LAB, WIDTH), F32),
            pltpu.VMEM((LAB, WIDTH), F32),
            pltpu.VMEM((2, LAB, WIDTH), BF16),
            pltpu.VMEM((LAB, 8 * GRP), F32),
            pltpu.VMEM((2, 2, LAB, 8 * GRP), BF16),
            pltpu.VMEM((LAB, WIDTH), F32),
            pltpu.VMEM(part, F32),
            pltpu.VMEM(part, F32),
            pltpu.VMEM(part, F32),
            pltpu.VMEM(part, BF16),
            pltpu.VMEM((2, 15, 16, WIDTH), BF16),
            pltpu.VMEM((2, 4, 8, 384), F32),
            pltpu.VMEM((2, 3, 8, 384), F32),
            pltpu.VMEM((2, 8, 384), F32),
            pltpu.VMEM((2, 3, 8, 384), F32),
            pltpu.VMEM((2, 2, 4, 8, 384), F32),
            dma((2, 2, 3)), dma((2, 2, 3)),
            dma((2, 4)), dma((2,)),
            dma((2, 2, NX)), dma((2, 2, NX)),
            dma((2,)), dma((2,)),
            dma((2, 15)), dma((2, 15)),
            dma((2, 3)), dma((2, 3)),
            dma((2, 3)), dma((2, 3)),
            dma((2, 15)), dma((2, 2, 4)),
            dma((4,)),
        ],
        compiler_params=pltpu.CompilerParams(
            collective_id=0, has_side_effects=True, vmem_limit_bytes=48 << 20
        ),
    )(pool_features, pool_labels, pool_counts.reshape(1, -1), batch_rows, weights, momentum)


def solution(mesh):
    in_specs = (
        P("rows", None),
        P("rows", None),
        P("rows"),
        P(None, "rows"),
        P(("rows", "labels"), None),
        P(("rows", "labels"), None),
    )
    out_specs = (P(("rows", "labels"), None), P(("rows", "labels"), None), P(None, "rows", None))
    return jax.shard_map(
        per_device, mesh=mesh, in_specs=in_specs, out_specs=out_specs, check_vma=False
    )
```

time: 596 us -> 79.6 us (0.13)
  waiting for transfers between devices: 485 us -> 0 us
  Pallas kernels: 0 us -> 70.3 us
  blocking collectives: 51.9 us -> 0 us
  local copies, waits for them, and re-layouts: 25.3 us -> 8.3 us
  between operations: 14.2 us -> 0.65 us
  other arithmetic: 12 us -> 0 us
  matrix products: 7.3 us -> 0 us
    psum x1 -> x0, waiting for transfers between devices: 473 us -> none  [feature_sums(): whole = lax.psum(jnp.concatenate(parts, axis=1), ('rows', 'labels'))]
    pallas_call x0 -> x1, Pallas kernels: none -> 70.3 us  [per_device(): pl.pallas_call(kernel, out_shape=(jax.ShapeDtypeStruct(weights.shape, F32...]
    all_gather x1 -> x0, blocking collectives: 51.9 us -> none  [side_by_side(): filled = lax.all_gather(both, axis, axis=dim, tiled=True)]
    slice x2 -> x0, local copies, waits for them, and re-layouts: 20 us -> none  [the longest x1 19.6 us: per_device(): all_counts[batch][:, None]]
    all_gather x1 -> x0, waiting for transfers between devices: 11.7 us -> none  [per_device(): lax.all_gather(pool_features[batch_rows], 'rows', axis=1, tiled=True)]
    reduce_or x1 -> x0, other arithmetic: 8.16 us -> none  [per_device(): targets = jnp.any(matched, axis=1).astype(jnp.float32)]
    dot_general x6 -> x0, matrix products: 7.3 us -> none  [the longest x2 3.72 us: per_device(): lax.dot_general(errors, features, (((0,), (0,)), ((), ())), preferred_ele...]
    unnamed x13 -> x14, local copies, waits for them, and re-layouts: 1.31 us -> 8.3 us
  transfers between devices with their start and end apart: 2 -> 0, of which waited for: 2 -> 0; matrix products, arithmetic and copies ran while one was open for 6% -> 0% of each run, Pallas kernels for 0% -> 0%
where the time goes in v1:
time: 79.6 us; the launch traced here: 79.3 us
  Pallas kernels  70.3 us (88%)
  local copies, waits for them, and re-layouts  8.3 us (10%)
    pallas_call x1, Pallas kernels, per_device(): pl.pallas_call(kernel, out_shape=(jax.ShapeDtypeStruct(weights.shape, F32...  70.3 us
    unnamed x14, local copies, waits for them, and re-layouts  8.3 us

profile of v1, /device:TPU:24, one launch (start us, length us, event | category | flops | bytes accessed | tf_op | source)
XLA Modules:
  0.0 79.3 jit_solution(11130556181895940740)
XLA Ops:
  0.6 0.8 %copy.9.labels = s32[128,16]{1,0:T(8,128)S(1)} copy(s32[128,16]{0,1:T(8,128)} %param.7) | data formatting | bytes 16384 | tf_op args[1]
  1.4 0.0 copy-start
  1.4 1.3 %copy-done = f32[384,768]{1,0:T(8,128)S(1)} copy-done((f32[384,768]{1,0:T(8,128)S(1)}, f32[384,768]{1,0:T(8,128)}, u32[]{:S(2)}) %copy-start) | copy-done | bytes 1179672
  2.7 0.0 copy-start.1
  2.7 1.3 %copy-done.1 = f32[384,768]{1,0:T(8,128)S(1)} copy-done((f32[384,768]{1,0:T(8,128)S(1)}, f32[384,768]{1,0:T(8,128)}, u32[]{:S(2)}) %copy-start.1) | copy-done | bytes 1179672
  4.0 0.0 copy-start.2
  4.0 0.9 %copy-done.2 = bf16[128,768]{1,0:T(8,128)(2,1)S(1)} copy-done((bf16[128,768]{1,0:T(8,128)(2,1)S(1)}, bf16[128,768]{1,0:T(8,128)(2,1)}, u32[]{:S(2)}) %copy-start.2) | copy-done | bytes 196632
  4.9 0.0 copy-start.3
  4.9 0.7 copy-done.3
  5.6 0.0 copy-start.4
  5.6 0.7 copy-done.4
  6.2 70.3 %shard_map.85 = (f32[384,768]{1,0:T(8,128)S(1)}, f32[384,768]{1,0:T(8,128)S(1)}, f32[2,32,768]{2,1,0:T(8,128)S(1)}) custom-call(bf16[128,768]{1,0:T(8,128)(2,1)S(1)} %copy-done.2, s32[128,16]{1,0:T(8,128)S(1)} %copy.9.labels, s32[1,128]{1,0:T(1,128)S(1)} %bitcast.1, s32[2,32]{1,0:T(2,128)S(1)} %copy-done.3, f32[384,768]{1,0:T(8,128)S(1)} %copy-done, ...), custom_call_target="tpu_custom_call" | custom-call | tf_op jit(solution)/shard_map/pallas_call | solution.py:344
  76.6 1.0 %copy.13 = f32[384,768]{1,0:T(8,128)} copy(f32[384,768]{1,0:T(8,128)S(1)} %get-tuple-element.6) | data formatting | bytes 2359296
  77.6 1.0 %copy.14 = f32[384,768]{1,0:T(8,128)} copy(f32[384,768]{1,0:T(8,128)S(1)} %get-tuple-element.7) | data formatting | bytes 2359296
  78.6 0.7 copy.15
Async XLA Ops:
  1.4 1.3 %copy-start = (f32[384,768]{1,0:T(8,128)S(1)}, f32[384,768]{1,0:T(8,128)}, u32[]{:S(2)}) copy-start(f32[384,768]{1,0:T(8,128)} %w_in.1) | copy-start | bytes 3538948
  2.7 1.3 %copy-start.1 = (f32[384,768]{1,0:T(8,128)S(1)}, f32[384,768]{1,0:T(8,128)}, u32[]{:S(2)}) copy-start(f32[384,768]{1,0:T(8,128)} %m_in.1) | copy-start | bytes 3538948
  4.0 0.9 %copy-start.2 = (bf16[128,768]{1,0:T(8,128)(2,1)S(1)}, bf16[128,768]{1,0:T(8,128)(2,1)}, u32[]{:S(2)}) copy-start(bf16[128,768]{1,0:T(8,128)(2,1)} %pool.1) | copy-start | bytes 589828
  4.9 0.7 copy-start.3
  5.6 0.7 copy-start.4

commit v2 on v1

--- a/solution.py
+++ b/solution.py
@@ -28,11 +28,11 @@
 
 
 def kernel(
-    pool, labels, counts, batch_rows, w_in, m_in,
-    w_out, m_out, fg_out,
-    feats, w, m, low, logits, errs, grads, own_part, other_part, core_in, chip_sum,
+    pool_in, labels_in, counts_in, rows_in, w_in, m_in,
+    w, m, fg_out,
+    pool, labels, counts, batch_rows, feats, low, logits, errs, grads, own_part, other_part, core_in, chip_sum,
     plane_in, quarter, line_in, line_sum, far_in, result,
-    x_send, x_recv, edge_send, edge_recv, core_send, core_recv, part_send, part_recv,
+    x_send, x_recv, edge_send, edge_recv, pair_send, pair_recv, core_send, core_recv, part_send, part_recv,
     plane_send, plane_recv, line_send, line_recv, far_send, far_recv, all_send, all_recv, local,
 ):
     rows_at, labels_at = lax.axis_index("rows"), lax.axis_index("labels")
@@ -42,7 +42,13 @@
     a, b = z >> 2, z & 3
     edge = (zl == 0) | (zl == 7)
     holder = zh == (y >> 1)
+    half = y & 1
+    piece = b ^ (a & 2)
     pending = []
+
+    def far_z(d):
+        to = (a + d) & 3
+        return to * 4 + (piece ^ (to & 2))
 
     def device(x=x, y=y, z=z, c=c):
         z = z & 15
@@ -69,6 +75,19 @@
 
     def arrived(dst, recv):
         remote(dst, dst, recv, recv, device(c=1 - c)).wait_recv()
+
+    load_w = pltpu.make_async_copy(w_in, w, local.at[0])
+    load_m = pltpu.make_async_copy(m_in, m, local.at[1])
+    small = [
+        pltpu.make_async_copy(src, dst, local.at[2 + i])
+        for i, (src, dst) in enumerate(
+            ((pool_in, pool), (labels_in, labels), (counts_in, counts), (rows_in, batch_rows))
+        )
+    ]
+    for copy in small:
+        copy.start()
+    load_w.start()
+    load_m.start()
 
     barrier = pltpu.get_barrier_semaphore()
 
@@ -93,19 +112,17 @@
     @pl.when(holder)
     def _():
         for d in range(1, 4):
-            greet(device(z=z + 4 * d))
-
-    load_w = pltpu.make_async_copy(w_in, w, local.at[0])
-    load_m = pltpu.make_async_copy(m_in, m, local.at[1])
-    load_w.start()
-    load_m.start()
-
+            greet(device(z=far_z(d)))
+
+
+    for copy in small:
+        copy.wait()
     lists = labels[...]
     tail = jnp.zeros((128, TAIL), F32)
     for d in range(3):
         digit = ((lists >> (6 * d)) & 63).astype(F32).astype(BF16)
         place = one_hot(iota((16, TAIL), 0) + 16 * d == iota((16, TAIL), 1))
-        tail = tail + dot(digit, place, ((1,), (0,)))
+        tail = tail + dot(digit, place, ((0,), (0,)))
     on_diagonal = iota((128, 128), 0) == iota((128, 128), 1)
     diagonal = jnp.where(on_diagonal, counts[...].astype(F32), 0.0).astype(BF16)
     tail = tail + dot(diagonal, one_hot(iota((128, TAIL), 1) == COUNT_LANE), ((1,), (0,)))
@@ -113,8 +130,9 @@
     for t in range(2):
         chosen = one_hot(iota((128, GRP), 0) == batch_rows[pl.ds(t, 1), :])
         own = feats.at[t, 0, 0, x]
-        own[:, :WIDTH] = dot(chosen, pool[...], ((0,), (0,))).astype(BF16)
-        own[:, WIDTH:] = dot(chosen, tail, ((0,), (0,))).astype(BF16)
+        features = dot(chosen, pool[...], ((0,), (0,))).astype(BF16)
+        own[:, :, :WIDTH] = features.reshape(2, 16, WIDTH)
+        own[:, :, WIDTH:] = dot(chosen, tail, ((0,), (0,))).astype(BF16).reshape(2, 16, TAIL)
 
     pl.semaphore_wait(
         barrier, 19 + jnp.where(holder, 16, 2) + jnp.where(edge, 4, 0)
@@ -124,37 +142,54 @@
         for k in (3, 2, 1, 0):
             to_z = jnp.where(zl == 0, z - 1 - k, z + 1 + k)
             start(
-                feats.at[t, 0, 0, x], feats.at[t, 1, 0, x],
+                feats.at[t, 0, 0, x, half], feats.at[t, 1, 0, x, half],
                 edge_send.at[t, k], edge_recv.at[t], device(z=to_z), when=edge,
             )
 
-    def send_core(t, far, at):
+    def send_core(*at):
         start(
-            feats.at[t, far, 0, at], feats.at[t, far, 1, at],
-            core_send.at[t, far, at], core_recv.at[t, far, at], device(c=1 - c),
+            feats.at[at[0], at[1], 0, *at[2:]], feats.at[at[0], at[1], 1, *at[2:]],
+            core_send.at[*at, *[0] * (4 - len(at))], core_recv.at[*at, *[0] * (4 - len(at))],
+            device(c=1 - c),
         )
 
-    def send_x(t, far):
+    def send_x(t):
         for d in (2, 1, 3):
             start(
-                feats.at[t, far, 0, x], feats.at[t, far, 0, x],
-                x_send.at[t, far, d - 1], x_recv.at[t, far, d - 1], device(x=(x + d) & 3),
-            )
-        send_core(t, far, x)
-
-    def pass_on(t, far):
+                feats.at[t, 0, 0, x], feats.at[t, 0, 0, x],
+                x_send.at[t, d - 1], x_recv.at[t, d - 1], device(x=(x + d) & 3),
+            )
+        send_core(t, 0, x)
+
+    def pass_near(t):
         for d in (1, 3, 2):
             at = (x - d) & 3
-            arrived(feats.at[t, far, 0, at], x_recv.at[t, far, d - 1])
-            send_core(t, far, at)
+            arrived(feats.at[t, 0, 0, at], x_recv.at[t, d - 1])
+            send_core(t, 0, at)
 
     def have_edge(t):
-        arrived(feats.at[t, 1, 0, x], edge_recv.at[t])
-        send_x(t, 1)
+        arrived(feats.at[t, 1, 0, x, half], edge_recv.at[t])
+        for q in (5, 4, 3, 7, 2, 6, 1):
+            start(
+                feats.at[t, 1, 0, x, half], feats.at[t, 1, 0, x, half],
+                pair_send.at[t, q - 1], pair_recv.at[t, q - 1],
+                device(x=(x + (q >> 1)) & 3, y=y ^ (q & 1)),
+            )
+        send_core(t, 1, x, half)
+
+    def pass_far(t):
+        for q in (1, 2, 6, 3, 7, 4, 5):
+            at = (x - (q >> 1)) & 3, half ^ (q & 1)
+            arrived(feats.at[t, 1, 0, *at], pair_recv.at[t, q - 1])
+            send_core(t, 1, *at)
 
     def have_core(t, far):
         for at in range(NX):
-            arrived(feats.at[t, far, 1, at], core_recv.at[t, far, at])
+            if far:
+                for i in range(2):
+                    arrived(feats.at[t, 1, 1, at, i], core_recv.at[t, 1, at, i])
+            else:
+                arrived(feats.at[t, 0, 1, at], core_recv.at[t, 0, at, 0])
 
     base = ((rows_at * 32 + labels_at) * LAB).astype(F32)
 
@@ -207,32 +242,33 @@
             both = jnp.concatenate([errs[t, 0, :, cols], errs[t, 1, :, cols]], axis=1)
             part = dot(both, low[t], ((0,), (0,))).reshape(2, NX, 2, 16, WIDTH)
             if other:
-                other_part[t] = part
-                start(
-                    other_part.at[t], core_in.at[t],
-                    part_send.at[t], part_recv.at[t], device(c=1 - c),
-                )
+                for at in range(NX):
+                    other_part[t, at] = part[:, at]
+                for d in (2, 1, 3, 0):
+                    at = (x + d) & 3
+                    start(
+                        other_part.at[t, at], core_in.at[t, at],
+                        part_send.at[t, at], part_recv.at[t, at], device(c=1 - c),
+                    )
             else:
-                own_part[t] = part
+                for at in range(NX):
+                    own_part[t, at] = part[:, at]
 
     def plane_start(t):
-        arrived(core_in.at[t], part_recv.at[t])
-
-        def chunk(i, _):
-            far, at = i >> 2, i & 3
-            chip_sum[t, far, at] = (own_part[t, far, at] + core_in[t, far, at]).astype(BF16)
-            return 0
-
-        lax.fori_loop(0, 8, chunk, 0)
-        for p in range(1, 16):
-            to_x, to_y = (x + (p >> 2)) & 3, (y + (p & 3)) & 3
-            start(
-                chip_sum.at[t, (to_y >> 1) ^ zh, to_x, to_y & 1], plane_in.at[t, p - 1],
-                plane_send.at[t, p - 1], plane_recv.at[t, p - 1], device(x=to_x, y=to_y),
-            )
+        for dx in (2, 1, 3, 0):
+            to_x = (x + dx) & 3
+            arrived(core_in.at[t, to_x], part_recv.at[t, to_x])
+            chip_sum[t, to_x] = (own_part[t, to_x] + core_in[t, to_x]).astype(BF16)
+            for dy in (2, 1, 3, 0):
+                p, to_y = 4 * dx + dy, (y + dy) & 3
+                if p:
+                    start(
+                        chip_sum.at[t, to_x, (to_y >> 1) ^ zh, to_y & 1], plane_in.at[t, p - 1],
+                        plane_send.at[t, p - 1], plane_recv.at[t, p - 1], device(x=to_x, y=to_y),
+                    )
 
     def line_start(t):
-        mine = (t, (y >> 1) ^ zh, x, y & 1)
+        mine = (t, x, (y >> 1) ^ zh, half)
         total = own_part[mine] + core_in[mine]
         for p in range(1, 16):
             arrived(plane_in.at[t, p - 1], plane_recv.at[t, p - 1])
@@ -240,15 +276,15 @@
             total = total + plane_in[t, p - 1].astype(F32)
         for k in range(4):
             quarter[t, k] = total[8 * (k >> 1) : 8 * (k >> 1) + 8, 384 * (k & 1) : 384 * (k & 1) + 384]
-        for d in range(1, 4):
+        for d in (2, 1, 3):
             to_b = (b + d) & 3
             start(
-                quarter.at[t, to_b], line_in.at[t, d - 1],
+                quarter.at[t, to_b ^ (a & 2)], line_in.at[t, d - 1],
                 line_send.at[t, d - 1], line_recv.at[t, d - 1], device(z=a * 4 + to_b),
             )
 
     def far_start(t):
-        total = quarter[t, b]
+        total = quarter[t, piece]
         for d in range(1, 4):
             arrived(line_in.at[t, d - 1], line_recv.at[t, d - 1])
             total = total + line_in[t, d - 1]
@@ -256,7 +292,7 @@
         for d in (2, 1, 3):
             start(
                 line_sum.at[t], far_in.at[t, d - 1], far_send.at[t, d - 1], far_recv.at[t, d - 1],
-                device(z=z + 4 * d), when=(((a + d) & 3) >> 1) == (y >> 1),
+                device(z=far_z(d)), when=(((a + d) & 3) >> 1) == (y >> 1),
             )
 
     def all_start(t):
@@ -266,19 +302,19 @@
             for d in range(1, 4):
                 arrived(far_in.at[t, d - 1], far_recv.at[t, d - 1])
                 total = total + far_in[t, d - 1]
-            result[t, y & 1, b] = total
+            result[t, half, piece] = total
 
         for q in range(15, 0, -1):
             start(
-                result.at[t, y & 1, b], result.at[t, y & 1, b],
-                all_send.at[t, q - 1], all_recv.at[t, y & 1, b],
+                result.at[t, half, piece], result.at[t, half, piece],
+                all_send.at[t, q - 1], all_recv.at[t, half, piece],
                 device(y=(y + (q >> 2)) & 3, z=a * 4 + ((b + (q & 3)) & 3)), when=holder,
             )
 
     def finish(t):
         for i in range(2):
             for k in range(4):
-                mine = holder & (i == (y & 1)) & (k == b)
+                mine = holder & (i == half) & (k == piece)
 
                 @pl.when(jnp.logical_not(mine))
                 def _():
@@ -290,18 +326,18 @@
                 fg_out[t, r : r + 8, s : s + 384] = result[t, i, k]
 
     send_edge(0)
-    send_x(0, 0)
-    send_x(1, 0)
+    send_x(0)
+    send_edge(1)
+    send_x(1)
     load_w.wait()
     load_m.wait()
     low[0] = w[...].astype(BF16)
-    pass_on(0, 0)
-    send_edge(1)
+    pass_near(0)
     have_edge(0)
     have_core(0, 0)
     block_errors(0, 0)
-    pass_on(1, 0)
-    pass_on(0, 1)
+    pass_near(1)
+    pass_far(0)
     have_core(0, 1)
     block_errors(0, 1)
     update(0)
@@ -309,18 +345,14 @@
     products(0)
     have_core(1, 0)
     block_errors(1, 0)
-    pass_on(1, 1)
+    pass_far(1)
     plane_start(0)
     have_core(1, 1)
     block_errors(1, 1)
     products(1)
+    plane_start(1)
     line_start(0)
-    plane_start(1)
     update(1)
-    store_w = pltpu.make_async_copy(w, w_out, local.at[2])
-    store_m = pltpu.make_async_copy(m, m_out, local.at[3])
-    store_w.start()
-    store_m.start()
     far_start(0)
     line_start(1)
     all_start(0)
@@ -333,27 +365,40 @@
             done()
         else:
             pl.when(when)(done)
-    store_w.wait()
-    store_m.wait()
+
+
+def store(w, m, fg, w_out, m_out, fg_out, sems):
+    copies = [pltpu.make_async_copy(fg, fg_out, sems.at[0])]
+    for src, dst in ((w, w_out), (m, m_out)):
+        for i in range(4):
+            at = pl.ds(i * (LAB // 4), LAB // 4)
+            copies.append(pltpu.make_async_copy(src.at[at], dst.at[at], sems.at[len(copies)]))
+    for copy in copies:
+        copy.start()
+    for copy in copies:
+        copy.wait()
 
 
 def per_device(pool_features, pool_labels, pool_counts, batch_rows, weights, momentum):
-    vmem, anywhere = pl.BlockSpec(memory_space=pltpu.VMEM), pl.BlockSpec(memory_space=pl.ANY)
+    vmem, hbm = pl.BlockSpec(memory_space=pltpu.VMEM), pl.BlockSpec(memory_space=pltpu.HBM)
     dma = pltpu.SemaphoreType.DMA
-    part = (2, 2, NX, 2, 16, WIDTH)
-    return pl.pallas_call(
+    part = (2, NX, 2, 2, 16, WIDTH)
+    shapes = (
+        jax.ShapeDtypeStruct(weights.shape, F32),
+        jax.ShapeDtypeStruct(momentum.shape, F32),
+        jax.ShapeDtypeStruct((2, GRP, WIDTH), F32),
+    )
+    results = pl.pallas_call(
         kernel,
-        out_shape=(
-            jax.ShapeDtypeStruct(weights.shape, F32),
-            jax.ShapeDtypeStruct(momentum.shape, F32),
-            jax.ShapeDtypeStruct((2, GRP, WIDTH), F32),
-        ),
-        in_specs=[vmem, vmem, vmem, vmem, anywhere, anywhere],
-        out_specs=(anywhere, anywhere, vmem),
+        out_shape=tuple(pltpu.VMEM(s.shape, s.dtype) for s in shapes),
+        in_specs=[hbm] * 6,
+        out_specs=(vmem, vmem, vmem),
         scratch_shapes=[
-            pltpu.VMEM((2, 2, 2, NX, GRP, FULL), BF16),
-            pltpu.VMEM((LAB, WIDTH), F32),
-            pltpu.VMEM((LAB, WIDTH), F32),
+            pltpu.VMEM((128, WIDTH), BF16),
+            pltpu.VMEM((16, 128), jnp.int32),
+            pltpu.VMEM((1, 128), jnp.int32),
+            pltpu.VMEM((2, GRP), jnp.int32),
+            pltpu.VMEM((2, 2, 2, NX, 2, 16, FULL), BF16),
             pltpu.VMEM((2, LAB, WIDTH), BF16),
             pltpu.VMEM((LAB, 8 * GRP), F32),
             pltpu.VMEM((2, 2, LAB, 8 * GRP), BF16),
@@ -368,20 +413,36 @@
             pltpu.VMEM((2, 8, 384), F32),
             pltpu.VMEM((2, 3, 8, 384), F32),
             pltpu.VMEM((2, 2, 4, 8, 384), F32),
-            dma((2, 2, 3)), dma((2, 2, 3)),
+            dma((2, 3)), dma((2, 3)),
             dma((2, 4)), dma((2,)),
-            dma((2, 2, NX)), dma((2, 2, NX)),
-            dma((2,)), dma((2,)),
+            dma((2, 7)), dma((2, 7)),
+            dma((2, 2, NX, 2)), dma((2, 2, NX, 2)),
+            dma((2, NX)), dma((2, NX)),
             dma((2, 15)), dma((2, 15)),
             dma((2, 3)), dma((2, 3)),
             dma((2, 3)), dma((2, 3)),
             dma((2, 15)), dma((2, 2, 4)),
-            dma((4,)),
+            dma((6,)),
         ],
         compiler_params=pltpu.CompilerParams(
             collective_id=0, has_side_effects=True, vmem_limit_bytes=48 << 20
         ),
-    )(pool_features, pool_labels, pool_counts.reshape(1, -1), batch_rows, weights, momentum)
+    )(
+        *(
+            pltpu.with_memory_space_constraint(array, pltpu.HBM)
+            for array in (
+                pool_features, pool_labels.T, pool_counts.reshape(1, -1), batch_rows,
+                weights, momentum,
+            )
+        )
+    )
+    return pl.pallas_call(
+        store,
+        out_shape=shapes,
+        in_specs=[vmem] * 3,
+        out_specs=(hbm,) * 3,
+        scratch_shapes=[dma((9,))],
+    )(*(pltpu.with_memory_space_constraint(array, pltpu.VMEM) for array in results))
 
 
 def solution(mesh):

time: 79.6 us -> 69.7 us (0.88)
  local copies, waits for them, and re-layouts: 8.3 us -> 0 us
  Pallas kernels: 70.3 us -> 68.2 us
    unnamed x14 -> x0, local copies, waits for them, and re-layouts: 8.3 us -> none
    pallas_call x1 -> x2, Pallas kernels: 70.3 us -> 68.2 us  [the longest x1 66.7 us: per_device(): pl.pallas_call(kernel, out_shape=tuple((pltpu.VMEM(s.shape, s.dtype) for...]
where the time goes in v2:
time: 69.7 us; the launch traced here: 68.9 us
  Pallas kernels  68.2 us (98%)
    pallas_call x1, Pallas kernels, per_device(): pl.pallas_call(kernel, out_shape=tuple((pltpu.VMEM(s.shape, s.dtype) for...  66.7 us
    pallas_call x1, Pallas kernels, per_device(): pl.pallas_call(store, out_shape=shapes, in_specs=[vmem] * 3, out_specs=(h...  1.54 us

profile of v2, /device:TPU:24, one launch (start us, length us, event | category | flops | bytes accessed | tf_op | source)
XLA Modules:
  0.0 68.9 jit_solution(15402315537352167437)
XLA Ops:
  0.6 66.7 %shard_map.85 = (f32[384,768]{1,0:T(8,128)S(1)}, f32[384,768]{1,0:T(8,128)S(1)}, f32[2,32,768]{2,1,0:T(8,128)S(1)}) custom-call(bf16[128,768]{1,0:T(8,128)(2,1)} %pool_in.1, s32[16,128]{1,0:T(8,128)} %bitcast.2, s32[1,128]{1,0:T(1,128)} %bitcast.3, s32[2,32]{1,0:T(2,128)} %rows_in.1, f32[384,768]{1,0:T(8,128)} %w_in.1, f32[384,768]{1,0:T(8,128)} %m_in.1), custom_call_target="tpu_custom_call" | custom-call | tf_op jit(solution)/shard_map/pallas_call | solution.py:391
  67.3 1.5 %shard_map.86 = (f32[384,768]{1,0:T(8,128)}, f32[384,768]{1,0:T(8,128)}, f32[2,32,768]{2,1,0:T(8,128)}) custom-call(f32[384,768]{1,0:T(8,128)S(1)} %get-tuple-element.6.w, f32[384,768]{1,0:T(8,128)S(1)} %get-tuple-element.7.m, f32[2,32,768]{2,1,0:T(8,128)S(1)} %get-tuple-element.8.fg), custom_call_target="tpu_custom_call" | custom-call | tf_op jit(solution)/shard_map/pallas_call | solution.py:439

commit v3 on v2

--- a/solution.py
+++ b/solution.py
@@ -30,7 +30,7 @@
 def kernel(
     pool_in, labels_in, counts_in, rows_in, w_in, m_in,
     w, m, fg_out,
-    pool, labels, counts, batch_rows, feats, low, logits, errs, grads, own_part, other_part, core_in, chip_sum,
+    pool, labels, counts, batch_rows, feats0, feats1, low, logits, errs, grads, own_part, other_part, core_in, chip_sum,
     plane_in, quarter, line_in, line_sum, far_in, result,
     x_send, x_recv, edge_send, edge_recv, pair_send, pair_recv, core_send, core_recv, part_send, part_recv,
     plane_send, plane_recv, line_send, line_recv, far_send, far_recv, all_send, all_recv, local,
@@ -41,10 +41,11 @@
     z = zh * 8 + zl
     a, b = z >> 2, z & 3
     edge = (zl == 0) | (zl == 7)
-    holder = zh == (y >> 1)
-    half = y & 1
+    holder = zh == (y & 1)
+    half, part = y & 1, y >> 1
     piece = b ^ (a & 2)
     pending = []
+    feats = (feats0, feats1)
 
     def far_z(d):
         to = (a + d) & 3
@@ -94,26 +95,28 @@
     def greet(to):
         pl.semaphore_signal(barrier, inc=1, device_id=to, device_id_type=MESH)
 
-    source_z = jnp.where(zl < 4, zh * 8 + 15, zh * 8 + 8)
-    greet(device(z=source_z))
-    greet(device(c=1 - c))
-    for p in range(1, 16):
-        greet(device(x=(x + (p >> 2)) & 3, y=(y + (p & 3)) & 3))
-    for d in range(1, 4):
-        greet(device(z=a * 4 + ((b + d) & 3)))
-    for i in range(2):
-        for k in range(4):
-            from_y = 2 * zh + i
+    @pl.when(holder)
+    def _():
+        for d in (2, 1, 3):
+            greet(device(z=far_z(d)))
+
+    for k in range(4):
+        for i in range(2):
+            from_y = zh + 2 * i
 
             @pl.when((from_y != y) | (k != b))
             def _():
                 greet(device(y=from_y, z=a * 4 + k))
 
-    @pl.when(holder)
-    def _():
-        for d in range(1, 4):
-            greet(device(z=far_z(d)))
-
+    for dx in (2, 1, 3, 0):
+        for dy in (2, 1, 3, 0):
+            if dx or dy:
+                greet(device(x=(x + dx) & 3, y=(y + dy) & 3))
+    source_z = jnp.where(zl < 4, zh * 8 + 15, zh * 8 + 8)
+    greet(device(z=source_z))
+    for d in range(1, 4):
+        greet(device(z=a * 4 + ((b + d) & 3)))
+    greet(device(c=1 - c))
 
     for copy in small:
         copy.wait()
@@ -121,18 +124,22 @@
     tail = jnp.zeros((128, TAIL), F32)
     for d in range(3):
         digit = ((lists >> (6 * d)) & 63).astype(F32).astype(BF16)
-        place = one_hot(iota((16, TAIL), 0) + 16 * d == iota((16, TAIL), 1))
+        lane = iota((16, TAIL), 1) & 63
+        place = one_hot(iota((16, TAIL), 0) + 16 * d == lane)
         tail = tail + dot(digit, place, ((0,), (0,)))
     on_diagonal = iota((128, 128), 0) == iota((128, 128), 1)
     diagonal = jnp.where(on_diagonal, counts[...].astype(F32), 0.0).astype(BF16)
-    tail = tail + dot(diagonal, one_hot(iota((128, TAIL), 1) == COUNT_LANE), ((1,), (0,)))
-    tail = tail.astype(BF16)
+    at_count = one_hot((iota((128, TAIL), 1) & 63) == COUNT_LANE)
+    tail = (tail + dot(diagonal, at_count, ((1,), (0,)))).astype(BF16)
+    chosen = [
+        one_hot(iota((128, GRP), 0) == batch_rows[pl.ds(t, 1), :]) for t in range(2)
+    ]
     for t in range(2):
-        chosen = one_hot(iota((128, GRP), 0) == batch_rows[pl.ds(t, 1), :])
-        own = feats.at[t, 0, 0, x]
-        features = dot(chosen, pool[...], ((0,), (0,))).astype(BF16)
-        own[:, :, :WIDTH] = features.reshape(2, 16, WIDTH)
-        own[:, :, WIDTH:] = dot(chosen, tail, ((0,), (0,))).astype(BF16).reshape(2, 16, TAIL)
+        features = dot(chosen[t], pool[...], ((0,), (0,))).astype(BF16)
+        feats[t][0, 0, x, :, :, :WIDTH] = features.reshape(2, 16, WIDTH)
+    lists = [dot(chosen[t], tail, ((0,), (0,))) for t in range(2)]
+    lists = jnp.where(iota((GRP, TAIL), 1) < 64, lists[0], lists[1]).astype(BF16)
+    feats0[0, 0, x, :, :, WIDTH:] = lists.reshape(2, 16, TAIL)
 
     pl.semaphore_wait(
         barrier, 19 + jnp.where(holder, 16, 2) + jnp.where(edge, 4, 0)
@@ -142,13 +149,13 @@
         for k in (3, 2, 1, 0):
             to_z = jnp.where(zl == 0, z - 1 - k, z + 1 + k)
             start(
-                feats.at[t, 0, 0, x, half], feats.at[t, 1, 0, x, half],
+                feats[t].at[0, 0, x, half], feats[t].at[1, 0, x, half],
                 edge_send.at[t, k], edge_recv.at[t], device(z=to_z), when=edge,
             )
 
     def send_core(*at):
         start(
-            feats.at[at[0], at[1], 0, *at[2:]], feats.at[at[0], at[1], 1, *at[2:]],
+            feats[at[0]].at[at[1], 0, *at[2:]], feats[at[0]].at[at[1], 1, *at[2:]],
             core_send.at[*at, *[0] * (4 - len(at))], core_recv.at[*at, *[0] * (4 - len(at))],
             device(c=1 - c),
         )
@@ -156,7 +163,7 @@
     def send_x(t):
         for d in (2, 1, 3):
             start(
-                feats.at[t, 0, 0, x], feats.at[t, 0, 0, x],
+                feats[t].at[0, 0, x], feats[t].at[0, 0, x],
                 x_send.at[t, d - 1], x_recv.at[t, d - 1], device(x=(x + d) & 3),
             )
         send_core(t, 0, x)
@@ -164,14 +171,14 @@
     def pass_near(t):
         for d in (1, 3, 2):
             at = (x - d) & 3
-            arrived(feats.at[t, 0, 0, at], x_recv.at[t, d - 1])
+            arrived(feats[t].at[0, 0, at], x_recv.at[t, d - 1])
             send_core(t, 0, at)
 
     def have_edge(t):
-        arrived(feats.at[t, 1, 0, x, half], edge_recv.at[t])
+        arrived(feats[t].at[1, 0, x, half], edge_recv.at[t])
         for q in (5, 4, 3, 7, 2, 6, 1):
             start(
-                feats.at[t, 1, 0, x, half], feats.at[t, 1, 0, x, half],
+                feats[t].at[1, 0, x, half], feats[t].at[1, 0, x, half],
                 pair_send.at[t, q - 1], pair_recv.at[t, q - 1],
                 device(x=(x + (q >> 1)) & 3, y=y ^ (q & 1)),
             )
@@ -180,24 +187,24 @@
     def pass_far(t):
         for q in (1, 2, 6, 3, 7, 4, 5):
             at = (x - (q >> 1)) & 3, half ^ (q & 1)
-            arrived(feats.at[t, 1, 0, *at], pair_recv.at[t, q - 1])
+            arrived(feats[t].at[1, 0, *at], pair_recv.at[t, q - 1])
             send_core(t, 1, *at)
 
     def have_core(t, far):
         for at in range(NX):
             if far:
                 for i in range(2):
-                    arrived(feats.at[t, 1, 1, at, i], core_recv.at[t, 1, at, i])
+                    arrived(feats[t].at[1, 1, at, i], core_recv.at[t, 1, at, i])
             else:
-                arrived(feats.at[t, 0, 1, at], core_recv.at[t, 0, at, 0])
+                arrived(feats[t].at[0, 1, at], core_recv.at[t, 0, at, 0])
 
     base = ((rows_at * 32 + labels_at) * LAB).astype(F32)
 
     def block_errors(t, far):
-        block = feats[t, far].reshape(8 * GRP, FULL)
-        features, lists = block[:, :WIDTH], block[:, WIDTH:]
+        features = feats[t][far, :, :, :, :, :WIDTH].reshape(8 * GRP, WIDTH)
+        lists = feats0[far, :, :, :, :, WIDTH:].reshape(8 * GRP, TAIL)
         logits[...] = dot(low[t], features, ((1,), (1,)))
-        slot, lane = iota((16, TAIL), 0), iota((16, TAIL), 1)
+        slot, lane = iota((16, TAIL), 0), iota((16, TAIL), 1) - 64 * t
         weight = jnp.zeros((16, TAIL), F32)
         for d in range(3):
             weight = jnp.where(lane == slot + 16 * d, float(64**d), weight)
@@ -236,46 +243,47 @@
 
         lax.fori_loop(0, LAB // 64, chunk, 0)
 
-    def products(t):
+    def products(t, far):
         for other in (1, 0):
             cols = pl.ds(other * 128, 128)
-            both = jnp.concatenate([errs[t, 0, :, cols], errs[t, 1, :, cols]], axis=1)
-            part = dot(both, low[t], ((0,), (0,))).reshape(2, NX, 2, 16, WIDTH)
+            product = dot(errs[t, far, :, cols], low[t], ((0,), (0,)))
+            product = product.reshape(NX, 2, 16, WIDTH)
             if other:
-                for at in range(NX):
-                    other_part[t, at] = part[:, at]
+                other_part[t, far] = product
                 for d in (2, 1, 3, 0):
-                    at = (x + d) & 3
+                    at = t, far, (x + d) & 3
                     start(
-                        other_part.at[t, at], core_in.at[t, at],
-                        part_send.at[t, at], part_recv.at[t, at], device(c=1 - c),
+                        other_part.at[*at], core_in.at[*at],
+                        part_send.at[*at], part_recv.at[*at], device(c=1 - c),
                     )
             else:
-                for at in range(NX):
-                    own_part[t, at] = part[:, at]
-
-    def plane_start(t):
+                own_part[t, far] = product
+
+    def plane_start(t, far):
         for dx in (2, 1, 3, 0):
             to_x = (x + dx) & 3
-            arrived(core_in.at[t, to_x], part_recv.at[t, to_x])
-            chip_sum[t, to_x] = (own_part[t, to_x] + core_in[t, to_x]).astype(BF16)
-            for dy in (2, 1, 3, 0):
-                p, to_y = 4 * dx + dy, (y + dy) & 3
-                if p:
-                    start(
-                        chip_sum.at[t, to_x, (to_y >> 1) ^ zh, to_y & 1], plane_in.at[t, p - 1],
-                        plane_send.at[t, p - 1], plane_recv.at[t, p - 1], device(x=to_x, y=to_y),
-                    )
+            at = t, far, to_x
+            arrived(core_in.at[*at], part_recv.at[*at])
+            chip_sum[*at] = (own_part[*at] + core_in[*at]).astype(BF16)
+            for i in range(2):
+                to_y = (zh ^ far) + 2 * i
+                slot = 4 * dx + ((to_y - y) & 3)
+                start(
+                    chip_sum.at[*at, i], plane_in.at[t, slot],
+                    plane_send.at[t, far, 2 * dx + i], plane_recv.at[t, slot],
+                    device(x=to_x, y=to_y), when=None if dx else to_y != y,
+                )
 
     def line_start(t):
-        mine = (t, x, (y >> 1) ^ zh, half)
+        mine = (t, half ^ zh, x, part)
         total = own_part[mine] + core_in[mine]
         for p in range(1, 16):
-            arrived(plane_in.at[t, p - 1], plane_recv.at[t, p - 1])
+            arrived(plane_in.at[t, p], plane_recv.at[t, p])
         for p in range(1, 16):
-            total = total + plane_in[t, p - 1].astype(F32)
+            total = total + plane_in[t, p].astype(F32)
         for k in range(4):
-            quarter[t, k] = total[8 * (k >> 1) : 8 * (k >> 1) + 8, 384 * (k & 1) : 384 * (k & 1) + 384]
+            r, col = 8 * (k >> 1), 384 * (k & 1)
+            quarter[t, k] = total[r : r + 8, col : col + 384]
         for d in (2, 1, 3):
             to_b = (b + d) & 3
             start(
@@ -292,7 +300,7 @@
         for d in (2, 1, 3):
             start(
                 line_sum.at[t], far_in.at[t, d - 1], far_send.at[t, d - 1], far_recv.at[t, d - 1],
-                device(z=far_z(d)), when=(((a + d) & 3) >> 1) == (y >> 1),
+                device(z=far_z(d)), when=(((a + d) & 3) >> 1) == (y & 1),
             )
 
     def all_start(t):
@@ -302,28 +310,26 @@
             for d in range(1, 4):
                 arrived(far_in.at[t, d - 1], far_recv.at[t, d - 1])
                 total = total + far_in[t, d - 1]
-            result[t, half, piece] = total
+            result[t, part, piece] = total
 
         for q in range(15, 0, -1):
             start(
-                result.at[t, half, piece], result.at[t, half, piece],
-                all_send.at[t, q - 1], all_recv.at[t, half, piece],
+                result.at[t, part, piece], result.at[t, part, piece],
+                all_send.at[t, q - 1], all_recv.at[t, part, piece],
                 device(y=(y + (q >> 2)) & 3, z=a * 4 + ((b + (q & 3)) & 3)), when=holder,
             )
 
     def finish(t):
         for i in range(2):
             for k in range(4):
-                mine = holder & (i == half) & (k == piece)
+                mine = holder & (i == part) & (k == piece)
 
                 @pl.when(jnp.logical_not(mine))
                 def _():
                     arrived(result.at[t, i, k], all_recv.at[t, i, k])
 
-        for i in range(2):
-            for k in range(4):
-                r, s = 16 * i + 8 * (k >> 1), 384 * (k & 1)
-                fg_out[t, r : r + 8, s : s + 384] = result[t, i, k]
+                r, col = 16 * i + 8 * (k >> 1), 384 * (k & 1)
+                fg_out[t, r : r + 8, col : col + 384] = result[t, i, k]
 
     send_edge(0)
     send_x(0)
@@ -337,26 +343,30 @@
     have_core(0, 0)
     block_errors(0, 0)
     pass_near(1)
+    have_edge(1)
+    products(0, 0)
+    plane_start(0, 0)
     pass_far(0)
     have_core(0, 1)
     block_errors(0, 1)
     update(0)
-    have_edge(1)
-    products(0)
+    products(0, 1)
+    pass_far(1)
     have_core(1, 0)
     block_errors(1, 0)
-    pass_far(1)
-    plane_start(0)
+    plane_start(0, 1)
+    products(1, 0)
     have_core(1, 1)
     block_errors(1, 1)
-    products(1)
-    plane_start(1)
+    plane_start(1, 0)
+    products(1, 1)
+    plane_start(1, 1)
+    update(1)
     line_start(0)
-    update(1)
+    line_start(1)
     far_start(0)
-    line_start(1)
+    far_start(1)
     all_start(0)
-    far_start(1)
     all_start(1)
     finish(0)
     finish(1)
@@ -382,7 +392,7 @@
 def per_device(pool_features, pool_labels, pool_counts, batch_rows, weights, momentum):
     vmem, hbm = pl.BlockSpec(memory_space=pltpu.VMEM), pl.BlockSpec(memory_space=pltpu.HBM)
     dma = pltpu.SemaphoreType.DMA
-    part = (2, NX, 2, 2, 16, WIDTH)
+    part = (2, 2, NX, 2, 16, WIDTH)
     shapes = (
         jax.ShapeDtypeStruct(weights.shape, F32),
         jax.ShapeDtypeStruct(momentum.shape, F32),
@@ -398,7 +408,8 @@
             pltpu.VMEM((16, 128), jnp.int32),
             pltpu.VMEM((1, 128), jnp.int32),
             pltpu.VMEM((2, GRP), jnp.int32),
-            pltpu.VMEM((2, 2, 2, NX, 2, 16, FULL), BF16),
+            pltpu.VMEM((2, 2, NX, 2, 16, FULL), BF16),
+            pltpu.VMEM((2, 2, NX, 2, 16, WIDTH), BF16),
             pltpu.VMEM((2, LAB, WIDTH), BF16),
             pltpu.VMEM((LAB, 8 * GRP), F32),
             pltpu.VMEM((2, 2, LAB, 8 * GRP), BF16),
@@ -407,7 +418,7 @@
             pltpu.VMEM(part, F32),
             pltpu.VMEM(part, F32),
             pltpu.VMEM(part, BF16),
-            pltpu.VMEM((2, 15, 16, WIDTH), BF16),
+            pltpu.VMEM((2, 16, 16, WIDTH), BF16),
             pltpu.VMEM((2, 4, 8, 384), F32),
             pltpu.VMEM((2, 3, 8, 384), F32),
             pltpu.VMEM((2, 8, 384), F32),
@@ -417,8 +428,8 @@
             dma((2, 4)), dma((2,)),
             dma((2, 7)), dma((2, 7)),
             dma((2, 2, NX, 2)), dma((2, 2, NX, 2)),
-            dma((2, NX)), dma((2, NX)),
-            dma((2, 15)), dma((2, 15)),
+            dma((2, 2, NX)), dma((2, 2, NX)),
+            dma((2, 2, 8)), dma((2, 16)),
             dma((2, 3)), dma((2, 3)),
             dma((2, 3)), dma((2, 3)),
             dma((2, 15)), dma((2, 2, 4)),

time: 69.7 us -> 64.2 us (0.921)
  the two profiles are of different devices: /device:TPU:24 before, /device:TPU:1 now
where the time goes in v3:
time: 64.2 us; the launch traced here: 64 us
  Pallas kernels  63.4 us (99%)
    pallas_call x1, Pallas kernels, per_device(): pl.pallas_call(kernel, out_shape=tuple((pltpu.VMEM(s.shape, s.dtype) for...  61.9 us
    pallas_call x1, Pallas kernels, per_device(): pl.pallas_call(store, out_shape=shapes, in_specs=[vmem] * 3, out_specs=(h...  1.54 us

profile of v3, /device:TPU:1, one launch (start us, length us, event | category | flops | bytes accessed | tf_op | source)
XLA Modules:
  0.0 64.0 jit_solution(1817915650714811459)
XLA Ops:
  0.6 61.9 %shard_map.85 = (f32[384,768]{1,0:T(8,128)S(1)}, f32[384,768]{1,0:T(8,128)S(1)}, f32[2,32,768]{2,1,0:T(8,128)S(1)}) custom-call(bf16[128,768]{1,0:T(8,128)(2,1)} %pool_in.1, s32[16,128]{1,0:T(8,128)} %bitcast.2, s32[1,128]{1,0:T(1,128)} %bitcast.3, s32[2,32]{1,0:T(2,128)} %rows_in.1, f32[384,768]{1,0:T(8,128)} %w_in.1, f32[384,768]{1,0:T(8,128)} %m_in.1), custom_call_target="tpu_custom_call" | custom-call | tf_op jit(solution)/shard_map/pallas_call | solution.py:401
  62.5 1.5 %shard_map.86 = (f32[384,768]{1,0:T(8,128)}, f32[384,768]{1,0:T(8,128)}, f32[2,32,768]{2,1,0:T(8,128)}) custom-call(f32[384,768]{1,0:T(8,128)S(1)} %get-tuple-element.6.w, f32[384,768]{1,0:T(8,128)S(1)} %get-tuple-element.7.m, f32[2,32,768]{2,1,0:T(8,128)S(1)} %get-tuple-element.8.fg), custom_call_target="tpu_custom_call" | custom-call | tf_op jit(solution)/shard_map/pallas_call | solution.py:450

commit v4 on v3

--- a/solution.py
+++ b/solution.py
@@ -33,7 +33,7 @@
     pool, labels, counts, batch_rows, feats0, feats1, low, logits, errs, grads, own_part, other_part, core_in, chip_sum,
     plane_in, quarter, line_in, line_sum, far_in, result,
     x_send, x_recv, edge_send, edge_recv, pair_send, pair_recv, core_send, core_recv, part_send, part_recv,
-    plane_send, plane_recv, line_send, line_recv, far_send, far_recv, all_send, all_recv, local,
+    plane_send, plane_recv, line_send, line_recv, far_send, far_recv, all_send, all_recv, local, token,
 ):
     rows_at, labels_at = lax.axis_index("rows"), lax.axis_index("labels")
     zh, x, c = rows_at >> 3, (rows_at >> 1) & 3, rows_at & 1
@@ -41,6 +41,8 @@
     z = zh * 8 + zl
     a, b = z >> 2, z & 3
     edge = (zl == 0) | (zl == 7)
+    inner = (zl == 3) | (zl == 4)
+    next_line = zh * 8 + 7 - zl
     holder = zh == (y & 1)
     half, part = y & 1, y >> 1
     piece = b ^ (a & 2)
@@ -95,28 +97,18 @@
     def greet(to):
         pl.semaphore_signal(barrier, inc=1, device_id=to, device_id_type=MESH)
 
-    @pl.when(holder)
-    def _():
-        for d in (2, 1, 3):
-            greet(device(z=far_z(d)))
-
-    for k in range(4):
-        for i in range(2):
-            from_y = zh + 2 * i
-
-            @pl.when((from_y != y) | (k != b))
-            def _():
-                greet(device(y=from_y, z=a * 4 + k))
-
-    for dx in (2, 1, 3, 0):
-        for dy in (2, 1, 3, 0):
-            if dx or dy:
-                greet(device(x=(x + dx) & 3, y=(y + dy) & 3))
+    for d in (2, 1, 3):
+        greet(device(z=a * 4 + ((b + d) & 3)))
+    for d in (2, 1, 3):
+        greet(device(x=(x + d) & 3))
+        greet(device(y=(y + d) & 3))
     source_z = jnp.where(zl < 4, zh * 8 + 15, zh * 8 + 8)
     greet(device(z=source_z))
-    for d in range(1, 4):
-        greet(device(z=a * 4 + ((b + d) & 3)))
     greet(device(c=1 - c))
+
+    @pl.when(inner)
+    def _():
+        greet(device(z=next_line))
 
     for copy in small:
         copy.wait()
@@ -142,7 +134,7 @@
     feats0[0, 0, x, :, :, WIDTH:] = lists.reshape(2, 16, TAIL)
 
     pl.semaphore_wait(
-        barrier, 19 + jnp.where(holder, 16, 2) + jnp.where(edge, 4, 0)
+        barrier, 10 + jnp.where(edge, 4, 0) + jnp.where(inner, 1, 0)
     )
 
     def send_edge(t):
@@ -189,6 +181,28 @@
             at = (x - (q >> 1)) & 3, half ^ (q & 1)
             arrived(feats[t].at[1, 0, *at], pair_recv.at[t, q - 1])
             send_core(t, 1, *at)
+
+    def send_token():
+        @pl.when(inner)
+        def _():
+            pl.semaphore_signal(
+                token.at[0], inc=1, device_id=device(z=next_line), device_id_type=MESH
+            )
+
+    def pass_token():
+        @pl.when(inner)
+        def _():
+            pl.semaphore_wait(token.at[0], 1)
+            for d in (2, 1, 3):
+                pl.semaphore_signal(
+                    token.at[1], inc=1, device_id=device(z=a * 4 + ((b + d) & 3)),
+                    device_id_type=MESH,
+                )
+
+    def have_token():
+        @pl.when(jnp.logical_not(inner))
+        def _():
+            pl.semaphore_wait(token.at[1], 1)
 
     def have_core(t, far):
         for at in range(NX):
@@ -340,6 +354,7 @@
     low[0] = w[...].astype(BF16)
     pass_near(0)
     have_edge(0)
+    send_token()
     have_core(0, 0)
     block_errors(0, 0)
     pass_near(1)
@@ -347,6 +362,7 @@
     products(0, 0)
     plane_start(0, 0)
     pass_far(0)
+    pass_token()
     have_core(0, 1)
     block_errors(0, 1)
     update(0)
@@ -361,10 +377,11 @@
     plane_start(1, 0)
     products(1, 1)
     plane_start(1, 1)
+    line_start(0)
+    have_token()
+    far_start(0)
+    line_start(1)
     update(1)
-    line_start(0)
-    line_start(1)
-    far_start(0)
     far_start(1)
     all_start(0)
     all_start(1)
@@ -434,6 +451,7 @@
             dma((2, 3)), dma((2, 3)),
             dma((2, 15)), dma((2, 2, 4)),
             dma((6,)),
+            pltpu.SemaphoreType.REGULAR((2,)),
         ],
         compiler_params=pltpu.CompilerParams(
             collective_id=0, has_side_effects=True, vmem_limit_bytes=48 << 20

time: 64.2 us -> 61.9 us (0.964)
  the two profiles are of different devices: /device:TPU:1 before, /device:TPU:24 now
where the time goes in v4:
time: 61.9 us; the launch traced here: 60.7 us
  Pallas kernels  60.1 us (97%)
  between operations  0.64 us (1%)
    pallas_call x1, Pallas kernels, per_device(): pl.pallas_call(kernel, out_shape=tuple((pltpu.VMEM(s.shape, s.dtype) for...  58.5 us
    pallas_call x1, Pallas kernels, per_device(): pl.pallas_call(store, out_shape=shapes, in_specs=[vmem] * 3, out_specs=(h...  1.54 us

profile of v4, /device:TPU:24, one launch (start us, length us, event | category | flops | bytes accessed | tf_op | source)
XLA Modules:
  0.0 60.7 jit_solution(3686397823860517152)
XLA Ops:
  0.6 58.5 %shard_map.85 = (f32[384,768]{1,0:T(8,128)S(1)}, f32[384,768]{1,0:T(8,128)S(1)}, f32[2,32,768]{2,1,0:T(8,128)S(1)}) custom-call(bf16[128,768]{1,0:T(8,128)(2,1)} %pool_in.1, s32[16,128]{1,0:T(8,128)} %bitcast.2, s32[1,128]{1,0:T(1,128)} %bitcast.3, s32[2,32]{1,0:T(2,128)} %rows_in.1, f32[384,768]{1,0:T(8,128)} %w_in.1, f32[384,768]{1,0:T(8,128)} %m_in.1), custom_call_target="tpu_custom_call" | custom-call | tf_op jit(solution)/shard_map/pallas_call | solution.py:418
  59.2 1.5 %shard_map.86 = (f32[384,768]{1,0:T(8,128)}, f32[384,768]{1,0:T(8,128)}, f32[2,32,768]{2,1,0:T(8,128)}) custom-call(f32[384,768]{1,0:T(8,128)S(1)} %get-tuple-element.6.w, f32[384,768]{1,0:T(8,128)S(1)} %get-tuple-element.7.m, f32[2,32,768]{2,1,0:T(8,128)S(1)} %get-tuple-element.8.fg), custom_call_target="tpu_custom_call" | custom-call | tf_op jit(solution)/shard_map/pallas_call | solution.py:468

commit v5 on v4

--- a/solution.py
+++ b/solution.py
@@ -264,7 +264,7 @@
             product = product.reshape(NX, 2, 16, WIDTH)
             if other:
                 other_part[t, far] = product
-                for d in (2, 1, 3, 0):
+                for d in (1, 3, 2, 0):
                     at = t, far, (x + d) & 3
                     start(
                         other_part.at[*at], core_in.at[*at],
@@ -274,7 +274,7 @@
                 own_part[t, far] = product
 
     def plane_start(t, far):
-        for dx in (2, 1, 3, 0):
+        for dx in (1, 3, 2, 0):
             to_x = (x + dx) & 3
             at = t, far, to_x
             arrived(core_in.at[*at], part_recv.at[*at])
@@ -326,7 +326,10 @@
                 total = total + far_in[t, d - 1]
             result[t, part, piece] = total
 
-        for q in range(15, 0, -1):
+        def hops(q):
+            return 2 - abs((q >> 2) - 2) + 2 * ((q & 3) > 0)
+
+        for q in sorted(range(1, 16), key=hops, reverse=True):
             start(
                 result.at[t, part, piece], result.at[t, part, piece],
                 all_send.at[t, q - 1], all_recv.at[t, part, piece],

time: 61.9 us -> 60.9 us (0.984); the launches traced: 60.7 us -> 60.7 us
  no operation moved by 1% of the time
where the time goes in v5:
time: 60.9 us; the launch traced here: 60.7 us
  Pallas kernels  60.1 us (99%)
  between operations  0.64 us (1%)
    pallas_call x1, Pallas kernels, per_device(): pl.pallas_call(kernel, out_shape=tuple((pltpu.VMEM(s.shape, s.dtype) for...  58.5 us
    pallas_call x1, Pallas kernels, per_device(): pl.pallas_call(store, out_shape=shapes, in_specs=[vmem] * 3, out_specs=(h...  1.54 us

profile of v5, /device:TPU:24, one launch (start us, length us, event | category | flops | bytes accessed | tf_op | source)
XLA Modules:
  0.0 60.7 jit_solution(16358739363662757264)
XLA Ops:
  0.6 58.5 %shard_map.85 = (f32[384,768]{1,0:T(8,128)S(1)}, f32[384,768]{1,0:T(8,128)S(1)}, f32[2,32,768]{2,1,0:T(8,128)S(1)}) custom-call(bf16[128,768]{1,0:T(8,128)(2,1)} %pool_in.1, s32[16,128]{1,0:T(8,128)} %bitcast.2, s32[1,128]{1,0:T(1,128)} %bitcast.3, s32[2,32]{1,0:T(2,128)} %rows_in.1, f32[384,768]{1,0:T(8,128)} %w_in.1, f32[384,768]{1,0:T(8,128)} %m_in.1), custom_call_target="tpu_custom_call" | custom-call | tf_op jit(solution)/shard_map/pallas_call | solution.py:421
  59.2 1.5 %shard_map.86 = (f32[384,768]{1,0:T(8,128)}, f32[384,768]{1,0:T(8,128)}, f32[2,32,768]{2,1,0:T(8,128)}) custom-call(f32[384,768]{1,0:T(8,128)S(1)} %get-tuple-element.6.w, f32[384,768]{1,0:T(8,128)S(1)} %get-tuple-element.7.m, f32[2,32,768]{2,1,0:T(8,128)S(1)} %get-tuple-element.8.fg), custom_call_target="tpu_custom_call" | custom-call | tf_op jit(solution)/shard_map/pallas_call | solution.py:471

commit v6 on v5

--- a/solution.py
+++ b/solution.py
@@ -380,11 +380,11 @@
     plane_start(1, 0)
     products(1, 1)
     plane_start(1, 1)
+    update(1)
     line_start(0)
     have_token()
     far_start(0)
     line_start(1)
-    update(1)
     far_start(1)
     all_start(0)
     all_start(1)

time: 60.9 us -> 60.9 us (level)
  no operation moved by 1% of the time
where the time goes in v6:
time: 60.9 us; the launch traced here: 60.7 us
  Pallas kernels  60.1 us (99%)
  between operations  0.64 us (1%)
    pallas_call x1, Pallas kernels, per_device(): pl.pallas_call(kernel, out_shape=tuple((pltpu.VMEM(s.shape, s.dtype) for...  58.5 us
    pallas_call x1, Pallas kernels, per_device(): pl.pallas_call(store, out_shape=shapes, in_specs=[vmem] * 3, out_specs=(h...  1.54 us

profile of v6, /device:TPU:24, one launch (start us, length us, event | category | flops | bytes accessed | tf_op | source)
XLA Modules:
  0.0 60.7 jit_solution(16818412946810464310)
XLA Ops:
  0.6 58.5 %shard_map.85 = (f32[384,768]{1,0:T(8,128)S(1)}, f32[384,768]{1,0:T(8,128)S(1)}, f32[2,32,768]{2,1,0:T(8,128)S(1)}) custom-call(bf16[128,768]{1,0:T(8,128)(2,1)} %pool_in.1, s32[16,128]{1,0:T(8,128)} %bitcast.2, s32[1,128]{1,0:T(1,128)} %bitcast.3, s32[2,32]{1,0:T(2,128)} %rows_in.1, f32[384,768]{1,0:T(8,128)} %w_in.1, f32[384,768]{1,0:T(8,128)} %m_in.1), custom_call_target="tpu_custom_call" | custom-call | tf_op jit(solution)/shard_map/pallas_call | solution.py:421
  59.2 1.5 %shard_map.86 = (f32[384,768]{1,0:T(8,128)}, f32[384,768]{1,0:T(8,128)}, f32[2,32,768]{2,1,0:T(8,128)}) custom-call(f32[384,768]{1,0:T(8,128)S(1)} %get-tuple-element.6.w, f32[384,768]{1,0:T(8,128)S(1)} %get-tuple-element.7.m, f32[2,32,768]{2,1,0:T(8,128)S(1)} %get-tuple-element.8.fg), custom_call_target="tpu_custom_call" | custom-call | tf_op jit(solution)/shard_map/pallas_call | solution.py:471
